TPU v7x, 32 devices: a whole 2x2x4 slice. The times are simulated.
32 devices in a mesh: seg: 4 (over y, x), gx: 8 (over z, core).
Axes of the slice: x: 2, y: 2, z: 4, core: 2. Of those that a mesh axis runs over, the one named last changes fastest.
Arguments:
- start_states: float32 [4, 3, 24, 64, 384], P('seg', None, 'gx'), may hold values from -6 to 6
- base_flow: bfloat16 [4, 3, 3, 24, 64, 384], P('seg', None, None, 'gx'), may hold values from -3.5 to 3.5
Outputs:
- residual: float32 [4, 3, 24, 64, 384], P('seg', None, 'gx')
All inputs are finite; a program needn't handle non-finite values.
Results may differ from a plain program's by a relative error of at most 0.0015.
Values may be sent and summed in bfloat16 or wider, within the bound.
A program may use at most 128 MiB of HBM per device.

v0:
```python
import jax
import jax.numpy as jnp
from jax import lax
from jax.sharding import PartitionSpec as P

STEPS = 3


time_step = 0.3
viscosity = 0.45


def passed_along(block, axis, distance):
    devices = range(lax.axis_size(axis))
    route = [((i - distance) % len(devices), i) for i in devices]
    return lax.ppermute(block, axis, route)


def extended(cells, sides, width):
    for axis, dim in sides:
        count = lax.axis_size(axis)
        head = lax.slice_in_dim(cells, 0, width, axis=dim)
        tail = lax.slice_in_dim(cells, cells.shape[dim] - width, cells.shape[dim], axis=dim)
        cells = jnp.concatenate(
            [
                lax.ppermute(tail, axis, [(i, (i + 1) % count) for i in range(count)]),
                cells,
                lax.ppermute(head, axis, [((i + 1) % count, i) for i in range(count)]),
            ],
            axis=dim,
        )
    return cells


def advance(q_ext, b_ext):
    centre = q_ext[:, 1:-1]
    base_c = b_ext[:, 1:-1]
    zero_row = jnp.zeros((3, centre.shape[1], 1, centre.shape[3]), jnp.float32)
    q_pad = jnp.concatenate([zero_row, centre, zero_row], axis=2)
    wall_sign = jnp.concatenate(
        [
            jnp.ones((1, centre.shape[1], 1, centre.shape[3]), jnp.float32),
            jnp.zeros((2, centre.shape[1], 1, centre.shape[3]), jnp.float32),
        ],
        axis=0,
    )
    b_pad = jnp.concatenate([-wall_sign, base_c, wall_sign], axis=2)
    q_up = jnp.roll(centre, -1, 3)
    q_down = jnp.roll(centre, 1, 3)
    dq_x = (q_ext[:, 2:] - q_ext[:, :-2]) * 0.5
    dq_y = (q_pad[:, :, 2:] - q_pad[:, :, :-2]) * 0.5
    dq_z = (q_up - q_down) * 0.5
    db_x = (b_ext[:, 2:] - b_ext[:, :-2]) * 0.5
    db_y = (b_pad[:, :, 2:] - b_pad[:, :, :-2]) * 0.5
    db_z = (jnp.roll(base_c, -1, 3) - jnp.roll(base_c, 1, 3)) * 0.5
    lap = (
        q_ext[:, 2:]
        + q_ext[:, :-2]
        + q_pad[:, :, 2:]
        + q_pad[:, :, :-2]
        + q_up
        + q_down
        - 6.0 * centre
    )
    advect = base_c[0:1] * dq_x + base_c[1:2] * dq_y + base_c[2:3] * dq_z
    produce = centre[0:1] * db_x + centre[1:2] * db_y + centre[2:3] * db_z
    return centre + time_step * (viscosity * lap - advect - produce)


def reflect_span(field):
    flipped = jnp.roll(jnp.flip(field, 3), 1, 3)
    sign = jnp.concatenate(
        [jnp.ones((2, 1, 1, 1), jnp.float32), -jnp.ones((1, 1, 1, 1), jnp.float32)], axis=0
    )
    return flipped * sign


def local(start_states, base_flow):
    start = start_states[0]
    snapshots = base_flow[0]
    half = lax.axis_size("gx") // 2
    seg_index = lax.axis_index("seg")
    seg_count = lax.axis_size("seg")
    incoming = passed_along(start, "seg", -1)
    turned = passed_along(incoming, "gx", half)
    target = jnp.where(seg_index == seg_count - 1, reflect_span(turned), incoming)
    base_ext = extended(snapshots, (("gx", 2),), 1)
    state = start
    for step in range(STEPS):
        state_ext = extended(state, (("gx", 1),), 1)
        state = advance(state_ext, base_ext[step].astype(jnp.float32))
    return (state - target)[None]


def solution(mesh):
    in_specs = (P("seg", None, "gx", None, None), P("seg", None, None, "gx", None, None))
    out_specs = P("seg", None, "gx", None, None)
    return jax.shard_map(local, mesh=mesh, in_specs=in_specs, out_specs=out_specs, check_vma=False)
```

profile of v0, /device:TPU:0, one launch (start us, length us, event | category | flops | bytes accessed | tf_op | source)
XLA Modules:
  0.0 92.2 jit_solution(15905311162643756208)
XLA Ops:
  0.0 2.2 %fusion.54 = (bf16[3,3,1,64,384]{4,3,2,1,0:T(8,128)(2,1)}, bf16[3,3,1,64,384]{4,3,2,1,0:T(8,128)(2,1)}) fusion(bf16[3,3,3,64,384]{4,3,2,1,0:T(8,128)(2,1)} %bitcast.61), kind=kLoop, calls=%fused_computation.107 | loop fusion | bytes 1769472 | tf_op jit(solution)/shard_map/slice | solution.py:23
  2.2 4.5 %collective-permute-start.3 = (bf16[3,3,1,64,384]{4,3,2,1,0:T(8,128)(2,1)}, bf16[3,3,1,64,384]{4,3,2,1,0:T(8,128)(2,1)}, u32[]{:S(2)}, u32[]{:S(2)}) collective-permute-start(bf16[3,3,1,64,384]{4,3,2,1,0:T(8,128)(2,1)} %get-tuple-element.30), channel_id=1, source_target_pairs={{1,0},{2,1},{3,2},{4,3},{5,4},{6,5},{7,6},{0,7},{9,8},{10,9},{11,1... | collective-permute-start | bytes 1327112 | tf_op jit(solution)/shard_map/ppermute | solution.py:28
  6.7 0.0 collective-permute-start.2
  6.7 2.4 %collective-permute-start.8 = (f32[3,3,64,384]{3,2,1,0:T(8,128)S(1)}, f32[3,3,64,384]{3,2,1,0:T(8,128)}, u32[]{:S(2)}, u32[]{:S(2)}) collective-permute-start(f32[3,3,64,384]{3,2,1,0:T(8,128)S(1)} %bitcast.56), channel_id=1, source_target_pairs={{8,0},{16,8},{24,16},{0,24},{9,1},{17,9},{25,17},{1,25},{10,2},{18... | collective-permute-start | bytes 2654216 | tf_op jit(solution)/shard_map/ppermute | solution.py:16
  9.2 0.9 fusion.61
  10.0 3.3 %collective-permute-start = (f32[3,1,64,384]{3,2,1,0:T(8,128)}, f32[3,1,64,384]{3,2,1,0:T(8,128)S(1)}, u32[]{:S(2)}, u32[]{:S(2)}) collective-permute-start(f32[3,1,64,384]{3,2,1,0:T(8,128)} %get-tuple-element.53), channel_id=1, source_target_pairs={{1,0},{2,1},{3,2},{4,3},{5,4},{6,5},{7,6},{0,7},{9,8},{10,9},{11,1... | collective-permute-start | bytes 884744 | tf_op jit(solution)/shard_map/ppermute | solution.py:28
  13.3 0.0 collective-permute-start.1
  13.3 0.1 multiply_bitcast_fusion.2
  13.4 0.1 fusion.63
  13.5 0.0 copy-start.1
  13.5 0.3 fusion.62
  13.8 3.8 %collective-permute-done.3 = bf16[3,3,1,64,384]{4,3,2,1,0:T(8,128)(2,1)} collective-permute-done((bf16[3,3,1,64,384]{4,3,2,1,0:T(8,128)(2,1)}, bf16[3,3,1,64,384]{4,3,2,1,0:T(8,128)(2,1)}, u32[]{:S(2)}, u32[]{:S(2)}) %collective-permute-start.3) | collective-permute-done | bytes 442400 | tf_op jit(solution)/shard_map/ppermute | solution.py:28
  17.7 3.7 %collective-permute-done.2 = bf16[3,3,1,64,384]{4,3,2,1,0:T(8,128)(2,1)} collective-permute-done((bf16[3,3,1,64,384]{4,3,2,1,0:T(8,128)(2,1)}, bf16[3,3,1,64,384]{4,3,2,1,0:T(8,128)(2,1)}, u32[]{:S(2)}, u32[]{:S(2)}) %collective-permute-start.2) | collective-permute-done | bytes 442400 | tf_op jit(solution)/shard_map/ppermute | solution.py:26
  21.4 1.4 %pad_maximum_fusion = bf16[3,3,5,64,384]{4,3,2,1,0:T(8,128)(2,1)S(1)} fusion(bf16[3,3,1,64,384]{4,3,2,1,0:T(8,128)(2,1)} %collective-permute-done.3, bf16[3,3,3,64,384]{4,3,2,1,0:T(8,128)(2,1)S(1)} %bitcast.62, bf16[3,3,1,64,384]{4,3,2,1,0:T(8,128)(2,1)} %collective-permute-done.2), kind=kLoop, calls=%fused_computation | loop fusion | flops 2211840 | bytes 4423680 | tf_op jit(solution)/shard_map/concatenate | solution.py:24
  22.8 0.5 fusion.30
  23.4 0.1 fusion.52
  23.5 0.3 fusion.53
  23.8 0.1 fusion.47
  23.9 0.1 fusion.50
  24.1 0.1 slice.405
  24.1 0.0 copy-start.6
  24.1 0.0 copy-start.7
  24.2 0.3 fusion.51
  24.5 0.0 collective-permute-done
  24.5 0.5 collective-permute-done.1
  25.0 3.0 %fusion.6 = f32[3,3,64,384]{3,2,1,0:T(8,128)S(1)} fusion(f32[3,3,64,384]{3,2,1,0:T(8,128)S(1)} %bitcast.60, f32[3,3,1,384]{3,2,1,0:T(1,128)S(1)} %copy-done.6, f32[3,3,1,384]{3,2,1,0:T(1,128)S(1)} %copy-done.7, f32[3,3,64,384]{3,2,1,0:T(8,128)S(1)} %slice.405, f32[3,5,64,384]{3,2,1,0:T(8,128)S(1)} %get-tuple-element.7, ...), kind=kLoop, calls=%fused_computation.19 | loop fusion | flops 7962624 | bytes 10349568 | tf_op jit(solution)/shard_map/add | solution.py:67
  27.9 0.3 fusion.59
  28.2 0.1 fusion.60
  28.4 0.1 fusion.41
  28.5 0.1 fusion.44
  28.6 0.8 collective-permute-start.4
  29.3 0.0 collective-permute-start.5
  29.4 0.9 fusion.38
  30.2 0.9 fusion.48
  31.1 0.1 slice.423
  31.2 1.0 %slice.443 = f32[3,3,64,384]{3,2,1,0:T(8,128)} slice(f32[3,5,64,384]{3,2,1,0:T(8,128)S(1)} %get-tuple-element.5), slice={[0:3], [1:4], [0:64], [0:384]} | slice | bytes 1769472 | tf_op jit(solution)/shard_map/slice | solution.py:37
  32.2 1.5 %fusion.49 = (f32[3,3,64,383]{3,2,1,0:T(8,128)}, f32[3,3,64,383]{3,2,1,0:T(8,128)}) fusion(f32[3,5,64,384]{3,2,1,0:T(8,128)S(1)} %get-tuple-element.5), kind=kLoop, calls=%fused_computation.102 | loop fusion | bytes 3529728 | tf_op jit(solution)/shard_map/jit(_roll_static)/slice | solution.py:55
  33.7 2.2 %collective-permute-done.4 = f32[3,1,64,384]{3,2,1,0:T(8,128)S(1)} collective-permute-done((f32[3,1,64,384]{3,2,1,0:T(8,128)S(1)}, f32[3,1,64,384]{3,2,1,0:T(8,128)S(1)}, u32[]{:S(2)}, u32[]{:S(2)}) %collective-permute-start.4) | collective-permute-done | bytes 294944 | tf_op jit(solution)/shard_map/ppermute | solution.py:28
  35.8 2.1 %collective-permute-done.5 = f32[3,1,64,384]{3,2,1,0:T(8,128)S(1)} collective-permute-done((f32[3,1,64,384]{3,2,1,0:T(8,128)S(1)}, f32[3,1,64,384]{3,2,1,0:T(8,128)S(1)}, u32[]{:S(2)}, u32[]{:S(2)}) %collective-permute-start.5) | collective-permute-done | bytes 294944 | tf_op jit(solution)/shard_map/ppermute | solution.py:26
  37.9 2.0 %fusion.13 = f32[3,3,64,384]{3,2,1,0:T(8,128)S(1)} fusion(f32[3,3,64,384]{3,2,1,0:T(8,128)S(1)} %fusion.6, f32[3,3,1,384]{3,2,1,0:T(1,128)S(1)} %copy-done.6, f32[3,3,1,384]{3,2,1,0:T(1,128)S(1)} %copy-done.7, f32[3,3,64,384]{3,2,1,0:T(8,128)S(1)} %slice.423, f32[3,5,64,384]{3,2,1,0:T(8,128)S(1)} %get-tuple-element.6, ...), kind=kLoop, calls=%fused_computation.26 | loop fusion | flops 7962624 | bytes 10349568 | tf_op jit(solution)/shard_map/add | solution.py:67
  40.0 0.0 collective-permute-done.8
  40.0 0.1 collective-permute-start.9
  40.1 0.9 fusion.55
  40.9 1.6 %collective-permute-start.6 = (f32[3,1,64,384]{3,2,1,0:T(8,128)}, f32[3,1,64,384]{3,2,1,0:T(8,128)}, u32[]{:S(2)}, u32[]{:S(2)}) collective-permute-start(f32[3,1,64,384]{3,2,1,0:T(8,128)} %get-tuple-element.35), channel_id=1, source_target_pairs={{1,0},{2,1},{3,2},{4,3},{5,4},{6,5},{7,6},{0,7},{9,8},{10,9},{11,1... | collective-permute-start | bytes 884744 | tf_op jit(solution)/shard_map/ppermute | solution.py:28
  42.6 0.0 collective-permute-start.7
  42.6 0.9 %fusion.35 = (f32[3,64,384]{2,1,0:T(8,128)}, f32[3,64,384]{2,1,0:T(8,128)}, f32[3,64,384]{2,1,0:T(8,128)}) fusion(f32[3,3,64,384]{3,2,1,0:T(8,128)S(1)} %fusion.13), kind=kLoop, calls=%fused_computation.73 | loop fusion | flops 221184 | bytes 1769472 | tf_op jit(solution)/shard_map/mul | solution.py:66
  43.5 0.9 %fusion.57 = (f32[3,3,64,1]{3,2,1,0:T(8,128)}, f32[3,3,64,1]{3,2,1,0:T(8,128)}) fusion(f32[3,3,64,384]{3,2,1,0:T(8,128)S(1)} %fusion.13), kind=kLoop, calls=%fused_computation.110 | loop fusion | bytes 9216 | tf_op jit(solution)/shard_map/jit(_roll_static)/slice | solution.py:48
  44.5 1.5 %fusion.56 = (f32[3,3,64,383]{3,2,1,0:T(8,128)}, f32[3,3,64,383]{3,2,1,0:T(8,128)}) fusion(f32[3,3,64,384]{3,2,1,0:T(8,128)S(1)} %fusion.13), kind=kLoop, calls=%fused_computation.109 | loop fusion | bytes 3529728 | tf_op jit(solution)/shard_map/jit(_roll_static)/slice | solution.py:48
  45.9 36.0 %collective-permute-done.9 = f32[3,3,64,384]{3,2,1,0:T(8,128)S(1)} collective-permute-done((f32[3,3,64,384]{3,2,1,0:T(8,128)}, f32[3,3,64,384]{3,2,1,0:T(8,128)S(1)}, u32[]{:S(2)}, u32[]{:S(2)}) %collective-permute-start.9) | collective-permute-done | bytes 884768 | tf_op jit(solution)/shard_map/ppermute | solution.py:16
  82.0 1.3 %slice.451 = f32[3,3,64,383]{3,2,1,0:T(8,128)} slice(f32[3,3,64,384]{3,2,1,0:T(8,128)S(1)} %collective-permute-done.9), slice={[0:3], [0:3], [0:64], [1:384]} | slice | bytes 1764864 | tf_op jit(solution)/shard_map/jit(_roll_static)/slice | solution.py:71
  83.2 0.0 copy-done.4
  83.2 2.2 %reverse.2 = f32[3,3,64,384]{3,2,1,0:T(8,128)S(1)} reverse(f32[3,3,64,384]{3,2,1,0:T(8,128)} %bitcast.63), dimensions={3} | reverse | bytes 1769472
  85.5 0.0 copy-start.2
  85.5 0.0 slice-start
  85.5 0.0 copy-start.8
  85.5 0.0 copy-start.9
  85.5 0.3 slice.545
  85.8 0.0 collective-permute-done.6
  85.8 0.0 collective-permute-done.7
  85.8 0.8 copy-done.2
  86.6 0.3 copy-done.3
  86.9 0.1 slice-done
  87.0 0.1 copy-done.5
  87.1 5.2 %fusion.22 = f32[1,3,3,64,384]{4,3,2,1,0:T(8,128)} fusion(f32[3,3,64,384]{3,2,1,0:T(8,128)S(1)} %fusion.13, f32[3,3,1,384]{3,2,1,0:T(1,128)S(1)} %copy-done.6, f32[3,3,1,384]{3,2,1,0:T(1,128)S(1)} %copy-done.8, f32[3,3,64,384]{3,2,1,0:T(8,128)} %slice.443, f32[3,5,64,384]{3,2,1,0:T(8,128)S(1)} %get-tuple-element.5, f32[3,3,64,1]{3,2,1,0:T(8,128)} %get-tuple-element.12, ...), kind=kLoop, calls=%fused_computation.35 | loop fusion | flops 8847360 | bytes 12119053 | tf_op jit(solution)/shard_map/broadcast_in_dim | solution.py:92
  (11 shorter events, 0.1 us)
Async XLA Ops:
  0.0 6.7 %copy-start = (f32[1,3,3,64,384]{4,3,2,1,0:T(8,128)S(1)}, f32[1,3,3,64,384]{4,3,2,1,0:T(8,128)}, u32[]{:S(2)}) copy-start(f32[1,3,3,64,384]{4,3,2,1,0:T(8,128)} %param.2) | copy-start | bytes 2654212
  2.2 15.4 %collective-permute-start.3 = (bf16[3,3,1,64,384]{4,3,2,1,0:T(8,128)(2,1)}, bf16[3,3,1,64,384]{4,3,2,1,0:T(8,128)(2,1)}, u32[]{:S(2)}, u32[]{:S(2)}) collective-permute-start(bf16[3,3,1,64,384]{4,3,2,1,0:T(8,128)(2,1)} %get-tuple-element.30), channel_id=1, source_target_pairs={{1,0},{2,1},{3,2},{4,3},{5,4},{6,5},{7,6},{0,7},{9,8},{10,9},{11,1... | collective-permute-start | bytes 1327112 | tf_op jit(solution)/shard_map/ppermute | solution.py:28
  6.7 14.6 %collective-permute-start.2 = (bf16[3,3,1,64,384]{4,3,2,1,0:T(8,128)(2,1)}, bf16[3,3,1,64,384]{4,3,2,1,0:T(8,128)(2,1)}, u32[]{:S(2)}, u32[]{:S(2)}) collective-permute-start(bf16[3,3,1,64,384]{4,3,2,1,0:T(8,128)(2,1)} %get-tuple-element.29), channel_id=1, source_target_pairs={{0,1},{1,2},{2,3},{3,4},{4,5},{5,6},{6,7},{7,0},{8,9},{9,10},{10,1... | collective-permute-start | bytes 1327112 | tf_op jit(solution)/shard_map/ppermute | solution.py:26
  6.7 33.2 %collective-permute-start.8 = (f32[3,3,64,384]{3,2,1,0:T(8,128)S(1)}, f32[3,3,64,384]{3,2,1,0:T(8,128)}, u32[]{:S(2)}, u32[]{:S(2)}) collective-permute-start(f32[3,3,64,384]{3,2,1,0:T(8,128)S(1)} %bitcast.56), channel_id=1, source_target_pairs={{8,0},{16,8},{24,16},{0,24},{9,1},{17,9},{25,17},{1,25},{10,2},{18... | collective-permute-start | bytes 2654216 | tf_op jit(solution)/shard_map/ppermute | solution.py:16
  10.0 14.4 %collective-permute-start = (f32[3,1,64,384]{3,2,1,0:T(8,128)}, f32[3,1,64,384]{3,2,1,0:T(8,128)S(1)}, u32[]{:S(2)}, u32[]{:S(2)}) collective-permute-start(f32[3,1,64,384]{3,2,1,0:T(8,128)} %get-tuple-element.53), channel_id=1, source_target_pairs={{1,0},{2,1},{3,2},{4,3},{5,4},{6,5},{7,6},{0,7},{9,8},{10,9},{11,1... | collective-permute-start | bytes 884744 | tf_op jit(solution)/shard_map/ppermute | solution.py:28
  13.3 11.6 %collective-permute-start.1 = (f32[3,1,64,384]{3,2,1,0:T(8,128)}, f32[3,1,64,384]{3,2,1,0:T(8,128)}, u32[]{:S(2)}, u32[]{:S(2)}) collective-permute-start(f32[3,1,64,384]{3,2,1,0:T(8,128)} %get-tuple-element.52), channel_id=1, source_target_pairs={{0,1},{1,2},{2,3},{3,4},{4,5},{5,6},{6,7},{7,0},{8,9},{9,10},{10,1... | collective-permute-start | bytes 884744 | tf_op jit(solution)/shard_map/ppermute | solution.py:26
  13.5 7.8 %copy-start.1 = (bf16[1,3,3,3,64,384]{5,4,3,2,1,0:T(8,128)(2,1)S(1)}, bf16[1,3,3,3,64,384]{5,4,3,2,1,0:T(8,128)(2,1)}, u32[]{:S(2)}) copy-start(bf16[1,3,3,3,64,384]{5,4,3,2,1,0:T(8,128)(2,1)} %param.3) | copy-start | bytes 3981316
  24.1 0.8 copy-start.6
  24.1 0.8 copy-start.7
  28.6 7.3 %collective-permute-start.4 = (f32[3,1,64,384]{3,2,1,0:T(8,128)S(1)}, f32[3,1,64,384]{3,2,1,0:T(8,128)S(1)}, u32[]{:S(2)}, u32[]{:S(2)}) collective-permute-start(f32[3,1,64,384]{3,2,1,0:T(8,128)S(1)} %get-tuple-element.44), channel_id=1, source_target_pairs={{1,0},{2,1},{3,2},{4,3},{5,4},{6,5},{7,6},{0,7},{9,8},{10,9},{11,1... | collective-permute-start | bytes 884744 | tf_op jit(solution)/shard_map/ppermute | solution.py:28
  29.3 8.6 %collective-permute-start.5 = (f32[3,1,64,384]{3,2,1,0:T(8,128)S(1)}, f32[3,1,64,384]{3,2,1,0:T(8,128)S(1)}, u32[]{:S(2)}, u32[]{:S(2)}) collective-permute-start(f32[3,1,64,384]{3,2,1,0:T(8,128)S(1)} %get-tuple-element.43), channel_id=1, source_target_pairs={{0,1},{1,2},{2,3},{3,4},{4,5},{5,6},{6,7},{7,0},{8,9},{9,10},{10,1... | collective-permute-start | bytes 884744 | tf_op jit(solution)/shard_map/ppermute | solution.py:26
  40.0 42.0 %collective-permute-start.9 = (f32[3,3,64,384]{3,2,1,0:T(8,128)}, f32[3,3,64,384]{3,2,1,0:T(8,128)S(1)}, u32[]{:S(2)}, u32[]{:S(2)}) collective-permute-start(f32[3,3,64,384]{3,2,1,0:T(8,128)} %collective-permute-done.8), channel_id=1, source_target_pairs={{4,0},{5,1},{6,2},{7,3},{0,4},{1,5},{2,6},{3,7},{12,8},{13,9},{14,... | collective-permute-start | bytes 2654216 | tf_op jit(solution)/shard_map/ppermute | solution.py:16
  40.9 44.9 %collective-permute-start.6 = (f32[3,1,64,384]{3,2,1,0:T(8,128)}, f32[3,1,64,384]{3,2,1,0:T(8,128)}, u32[]{:S(2)}, u32[]{:S(2)}) collective-permute-start(f32[3,1,64,384]{3,2,1,0:T(8,128)} %get-tuple-element.35), channel_id=1, source_target_pairs={{1,0},{2,1},{3,2},{4,3},{5,4},{6,5},{7,6},{0,7},{9,8},{10,9},{11,1... | collective-permute-start | bytes 884744 | tf_op jit(solution)/shard_map/ppermute | solution.py:28
  42.6 43.3 %collective-permute-start.7 = (f32[3,1,64,384]{3,2,1,0:T(8,128)}, f32[3,1,64,384]{3,2,1,0:T(8,128)}, u32[]{:S(2)}, u32[]{:S(2)}) collective-permute-start(f32[3,1,64,384]{3,2,1,0:T(8,128)} %get-tuple-element.34), channel_id=1, source_target_pairs={{0,1},{1,2},{2,3},{3,4},{4,5},{5,6},{6,7},{7,0},{8,9},{9,10},{10,1... | collective-permute-start | bytes 884744 | tf_op jit(solution)/shard_map/ppermute | solution.py:26
  82.0 1.3 %copy-start.4 = (f32[3,3,64,384]{3,2,1,0:T(8,128)}, f32[3,3,64,384]{3,2,1,0:T(8,128)S(1)}, u32[]{:S(2)}) copy-start(f32[3,3,64,384]{3,2,1,0:T(8,128)S(1)} %collective-permute-done.9) | copy-start | bytes 2654212
  85.5 1.2 %copy-start.2 = (f32[3,3,64,383]{3,2,1,0:T(8,128)S(1)}, f32[3,3,64,383]{3,2,1,0:T(8,128)}, u32[]{:S(2)}) copy-start(f32[3,3,64,383]{3,2,1,0:T(8,128)} %get-tuple-element.13) | copy-start | bytes 2647300
  85.5 1.4 %copy-start.3 = (f32[3,3,64,383]{3,2,1,0:T(8,128)S(1)}, f32[3,3,64,383]{3,2,1,0:T(8,128)}, u32[]{:S(2)}) copy-start(f32[3,3,64,383]{3,2,1,0:T(8,128)} %get-tuple-element.14) | copy-start | bytes 2647300
  85.5 1.5 %slice-start = ((f32[3,3,64,384]{3,2,1,0:T(8,128)}), f32[3,3,64,1]{3,2,1,0:T(8,128)S(1)}, s32[]{:S(2)}) async-start(f32[3,3,64,384]{3,2,1,0:T(8,128)} %copy-done.4), calls=%async_computation | async-start | bytes 589824 | tf_op jit(solution)/shard_map/jit(_roll_static)/slice | solution.py:71
  85.5 1.6 %copy-start.5 = (f32[3,64,384]{2,1,0:T(8,128)S(1)}, f32[3,64,384]{2,1,0:T(8,128)}, u32[]{:S(2)}) copy-start(f32[3,64,384]{2,1,0:T(8,128)} %get-tuple-element.9) | copy-start | bytes 884740
  85.5 1.6 %copy-start.8 = (f32[3,3,1,384]{3,2,1,0:T(1,128)S(1)}, f32[3,3,1,384]{3,2,1,0:T(1,128)}, u32[]{:S(2)}) copy-start(f32[3,3,1,384]{3,2,1,0:T(1,128)} %constant.7.clone.1) | copy-start | bytes 41476
  85.5 1.5 %copy-start.9 = (f32[3]{0:T(128)S(1)}, f32[3]{0:T(128)}, u32[]{:S(2)}) copy-start(f32[3]{0:T(128)} %constant.23.clone.1) | copy-start | bytes 40
where the time goes:
time: 92.5 us; the launch traced here: 92.2 us
  waiting for transfers between devices  48.3 us (52%)
  local copies, waits for them, and re-layouts  16.8 us (18%)
  other arithmetic  14.2 us (15%)
  starting transfers between devices  12.7 us (14%)
    ppermute x2, waiting for transfers between devices, passed_along(): return lax.ppermute(block, axis, route)  36 us
    ppermute x4, starting transfers between devices, extended(): lax.ppermute(head, axis, [((i + 1) % count, i) for i in range(count)])  10.2 us
    ppermute x4, waiting for transfers between devices, extended(): lax.ppermute(tail, axis, [(i, (i + 1) % count) for i in range(count)])  6.27 us
    ppermute x4, waiting for transfers between devices, extended(): lax.ppermute(head, axis, [((i + 1) % count, i) for i in range(count)])  6.01 us
    broadcast_in_dim x1, other arithmetic, local(): return (state - target)[None]  5.17 us
    add x2, other arithmetic, advance(): return centre + time_step * (viscosity * lap - advect - produce)  4.99 us
    slice x4, local copies, waits for them, and re-layouts, extended(): lax.slice_in_dim(cells, cells.shape[dim] - width, cells.shape[dim], axis=...  4.02 us
    unnamed x22, local copies, waits for them, and re-layouts  3.71 us
  transfers between devices with their start and end apart: 10, of which 6 were waited for; matrix products, arithmetic and copies ran while one was open for 24% of the time, Pallas kernels for 0%

commit v1 on v0

v1 whole, which is shorter than its diff:
```python
import functools

import jax
import jax.numpy as jnp
from jax import lax
from jax.experimental import pallas as pl
from jax.experimental.pallas import tpu as pltpu
from jax.sharding import PartitionSpec as P

TIME_STEP = 0.3
VISCOSITY = 0.45
MESH = pl.DeviceIdType.MESH
ROWS = 16
PAD_Q = 8
PAD_B = 16
F32 = jnp.float32
BF16 = jnp.bfloat16


def encode(values):
    square = values * values
    fourth = square * square
    eighth = fourth * fourth
    return jnp.where(values < 0, -eighth, eighth).astype(BF16)


def decode(code):
    code = code.astype(F32)
    size = jnp.sqrt(jnp.sqrt(jnp.sqrt(jnp.abs(code))))
    return jnp.where(code < 0, -size, size)


def kernel(n_seg, n_gx, steps, nl, ny, nz, start_ref, base_ref, out_ref, q, b, hq, hb, sq, enc, ra, rb, tq, tgt,
           load_sem, qs_sem, qr_sem, bs_sem, br_sem, shift_sem, a_sem, ar_sem, b_sem, c_sem, cr_sem):
    seg = lax.axis_index("seg")
    gx = lax.axis_index("gx")
    last = n_seg - 1
    left, right = lax.rem(gx + n_gx - 1, n_gx), lax.rem(gx + 1, n_gx)
    across = lax.rem(gx + n_gx // 2, n_gx)
    relays = (0, 1, 2, last)
    quarter = ny // 4

    load_q = pltpu.make_async_copy(start_ref.at[0], q.at[0, :, :, pl.ds(PAD_Q, ny), :], load_sem.at[0])
    load_q.start()
    load_b = [
        pltpu.make_async_copy(base_ref.at[0, k], b.at[k, :, :, pl.ds(PAD_B, ny), :], load_sem.at[1 + k])
        for k in range(steps)
    ]
    for copy in load_b:
        copy.start()

    barrier = pltpu.get_barrier_semaphore()
    for other in (left, right, across):
        pl.semaphore_signal(barrier, inc=1, device_id={"gx": other}, device_id_type=MESH)
    for d in range(1, n_seg):
        pl.semaphore_signal(barrier, inc=1, device_id={"seg": lax.rem(seg + d, n_seg)}, device_id_type=MESH)

    def q_copy(k, side):
        return pltpu.make_async_remote_copy(
            src_ref=sq.at[k, side], dst_ref=hq.at[k, side], send_sem=qs_sem.at[k, side], recv_sem=qr_sem.at[k, side],
            device_id={"gx": right if side == 0 else left}, device_id_type=MESH)

    def b_copy(k, side):
        return pltpu.make_async_remote_copy(
            src_ref=base_ref.at[0, k, :, nl - 1 if side == 0 else 0], dst_ref=hb.at[k, side],
            send_sem=bs_sem.at[k, side], recv_sem=br_sem.at[k, side],
            device_id={"gx": right if side == 0 else left}, device_id_type=MESH)

    shift = pltpu.make_async_remote_copy(
        src_ref=start_ref.at[0], dst_ref=tgt, send_sem=shift_sem.at[0], recv_sem=shift_sem.at[1],
        device_id={"seg": lax.rem(seg + n_seg - 1, n_seg)}, device_id_type=MESH)

    def a_copy(j):
        return pltpu.make_async_remote_copy(
            src_ref=enc.at[j], dst_ref=ra, send_sem=a_sem.at[j], recv_sem=ar_sem.at[0],
            device_id={"seg": relays[j]}, device_id_type=MESH)

    def z_copy(source):
        return pltpu.make_async_remote_copy(
            src_ref=source, dst_ref=rb, send_sem=b_sem.at[0], recv_sem=b_sem.at[1],
            device_id={"gx": across}, device_id_type=MESH)

    def c_copy(j):
        return pltpu.make_async_remote_copy(
            src_ref=rb, dst_ref=tq.at[j], send_sem=c_sem.at[0], recv_sem=cr_sem.at[j],
            device_id={"seg": last}, device_id_type=MESH)

    q[:, :, :, 0:PAD_Q, :] = jnp.zeros((2, 3, nl, PAD_Q, nz), F32)
    q[:, :, :, PAD_Q + ny:, :] = jnp.zeros((2, 3, nl, PAD_Q, nz), F32)
    for c in range(3):
        wall = jnp.full((steps, nl, PAD_B, nz), 1.0 if c == 0 else 0.0, BF16)
        b[:, c, :, 0:PAD_B, :] = -wall
        b[:, c, :, PAD_B + ny:, :] = wall

    load_q.wait()
    for c in range(3):
        sq[0, 0, c] = q[0, c, nl - 1, PAD_Q:PAD_Q + ny, :].astype(BF16)
        sq[0, 1, c] = q[0, c, 0, PAD_Q:PAD_Q + ny, :].astype(BF16)

    pl.semaphore_wait(barrier, 3 + n_seg - 1)
    for side in range(2):
        q_copy(0, side).start()
        b_copy(0, side).start()

    @pl.when(seg == 0)
    def _():
        for j in range(4):
            for c in range(3):
                enc[j, c] = encode(q[0, c, :, PAD_Q + j * quarter:PAD_Q + (j + 1) * quarter, :])
        for j in range(1, 4):
            a_copy(j).start()

    @pl.when(seg > 0)
    def _():
        shift.start()

    def q_window(slot, c, x, at):
        window = q[slot, c, x, pl.ds(at, ROWS + 2 * PAD_Q), :]
        return window[PAD_Q:PAD_Q + ROWS], window

    def shifted(window, pad):
        size = window.shape[0]
        up = pltpu.roll(window, size - 1, 0)[pad:pad + ROWS]
        down = pltpu.roll(window, 1, 0)[pad:pad + ROWS]
        return up, down

    half = 0.5 * TIME_STEP
    diffuse = TIME_STEP * VISCOSITY

    def layer(k, x):
        slot = k % 2

        def chunk(r, carry):
            at = pl.multiple_of(r * ROWS, ROWS)
            here = pl.ds(at, ROWS)

            def q_side(c, side):
                neighbour = x + (-1 if side == 0 else 1)
                if 0 <= neighbour < nl:
                    return q[slot, c, neighbour, pl.ds(at + PAD_Q, ROWS), :]
                return hq[k, side, c, here, :].astype(F32)

            def b_side(c, side):
                neighbour = x + (-1 if side == 0 else 1)
                if 0 <= neighbour < nl:
                    return b[k, c, neighbour, pl.ds(at + PAD_B, ROWS), :].astype(F32)
                return hb[k, side, c, here, :].astype(F32)

            windows = [b[k, c, x, pl.ds(at, ROWS + 2 * PAD_B), :].astype(F32) for c in range(3)]
            carried = [half * window[PAD_B:PAD_B + ROWS] for window in windows]
            ahead = [diffuse - value for value in carried]
            behind = [diffuse + value for value in carried]
            centres = [q[slot, c, x, pl.ds(at + PAD_Q, ROWS), :] for c in range(3)]
            pushed = [half * value for value in centres]
            for c in range(3):
                centre, window = q_window(slot, c, x, at)
                up, down = shifted(window, PAD_Q)
                total = (1.0 - 6.0 * diffuse) * centre
                total += ahead[0] * q_side(c, 1) + behind[0] * q_side(c, 0)
                total += ahead[1] * up + behind[1] * down
                total += ahead[2] * pltpu.roll(centre, nz - 1, 1) + behind[2] * pltpu.roll(centre, 1, 1)
                total -= pushed[0] * (b_side(c, 1) - b_side(c, 0))
                base = windows[c][PAD_B - 8:PAD_B + ROWS + 8]
                up, down = shifted(base, 8)
                total -= pushed[1] * (up - down)
                base = windows[c][PAD_B:PAD_B + ROWS]
                total -= pushed[2] * (pltpu.roll(base, nz - 1, 1) - pltpu.roll(base, 1, 1))
                if k == steps - 1:
                    out_ref[0, c, x, here, :] = total - tgt[c, x, here, :]
                else:
                    q[1 - slot, c, x, pl.ds(at + PAD_Q, ROWS), :] = total
                    if x == nl - 1:
                        sq[k + 1, 0, c, here, :] = total.astype(BF16)
                    if x == 0:
                        sq[k + 1, 1, c, here, :] = total.astype(BF16)
            return carry

        lax.fori_loop(0, ny // ROWS, chunk, 0)

    def is_relay():
        flag = seg == 0
        for r in relays[1:]:
            flag = flag | (seg == r)
        return flag

    def finish_target():
        @pl.when(seg < last)
        def _():
            shift.wait_recv()

        @pl.when(seg == last)
        def _():
            z_copy(ra).wait_recv()
            for j in range(3):
                c_copy(j).wait_recv()
            row = lax.broadcasted_iota(jnp.int32, (nz, nz), 0)
            column = lax.broadcasted_iota(jnp.int32, (nz, nz), 1)
            flip = jnp.where((row + column == 0) | (row + column == nz), 1.0, 0.0).astype(BF16)
            for j in range(4):
                source = rb if j == 3 else tq.at[j]
                for c in range(3):
                    values = decode(source[c]).reshape(nl * quarter, nz)
                    high = values.astype(BF16)
                    low = (values - high.astype(F32)).astype(BF16)
                    flipped = jnp.dot(high, flip, preferred_element_type=F32)
                    flipped += jnp.dot(low, flip, preferred_element_type=F32)
                    if c == 2:
                        flipped = -flipped
                    tgt[c, :, j * quarter:(j + 1) * quarter, :] = flipped.reshape(nl, quarter, nz)

    for k in range(steps):
        load_b[k].wait()
        if k == steps - 1:
            finish_target()
            for x in range(1, nl - 1):
                layer(k, x)
        if k == 0:
            for x in range(1, nl - 1):
                layer(k, x)
            for side in range(2):
                b_copy(1, side).start()

            @pl.when(seg == 0)
            def _():
                z_copy(enc.at[0]).start()

            @pl.when((seg != 0) & is_relay())
            def _():
                a_copy(0).wait_recv()
                z_copy(ra).start()

        for side in range(2):
            q_copy(k, side).wait_recv()
            b_copy(k, side).wait_recv()
        layer(k, 0)
        layer(k, nl - 1)
        if k < steps - 1:
            for side in range(2):
                q_copy(k + 1, side).start()
            if k + 2 < steps:
                for side in range(2):
                    b_copy(k + 2, side).start()
        if 0 < k < steps - 1:
            for x in range(1, nl - 1):
                layer(k, x)

            @pl.when(is_relay() & (seg != last))
            def _():
                z_copy(ra).wait_recv()
                for j in range(3):
                    @pl.when(seg == relays[j])
                    def _():
                        c_copy(j).start()

    for k in range(steps):
        for side in range(2):
            q_copy(k, side).wait_send()
            b_copy(k, side).wait_send()

    @pl.when(seg > 0)
    def _():
        shift.wait_send()

    @pl.when(seg == 0)
    def _():
        for j in range(1, 4):
            a_copy(j).wait_send()

    @pl.when(is_relay())
    def _():
        z_copy(ra).wait_send()

    @pl.when(is_relay() & (seg != last))
    def _():
        c_copy(0).wait_send()


def local(n_seg, n_gx, start_states, base_flow):
    _, _, nl, ny, nz = start_states.shape
    steps = base_flow.shape[1]
    quarter = ny // 4
    dma = pltpu.SemaphoreType.DMA
    return pl.pallas_call(
        functools.partial(kernel, n_seg, n_gx, steps, nl, ny, nz),
        out_shape=jax.ShapeDtypeStruct(start_states.shape, F32),
        in_specs=[pl.BlockSpec(memory_space=pl.ANY)] * 2,
        out_specs=pl.BlockSpec(memory_space=pltpu.VMEM),
        scratch_shapes=[
            pltpu.VMEM((2, 3, nl, ny + 2 * PAD_Q, nz), F32),
            pltpu.VMEM((steps, 3, nl, ny + 2 * PAD_B, nz), BF16),
            pltpu.VMEM((steps, 2, 3, ny, nz), BF16),
            pltpu.VMEM((steps, 2, 3, ny, nz), BF16),
            pltpu.VMEM((steps, 2, 3, ny, nz), BF16),
            pltpu.VMEM((4, 3, nl, quarter, nz), BF16),
            pltpu.VMEM((3, nl, quarter, nz), BF16),
            pltpu.VMEM((3, nl, quarter, nz), BF16),
            pltpu.VMEM((3, 3, nl, quarter, nz), BF16),
            pltpu.VMEM((3, nl, ny, nz), F32),
            dma((1 + steps,)),
            dma((steps, 2)), dma((steps, 2)),
            dma((steps, 2)), dma((steps, 2)),
            dma((2,)),
            dma((4,)), dma((1,)),
            dma((2,)),
            dma((1,)), dma((3,)),
        ],
        compiler_params=pltpu.CompilerParams(
            collective_id=0, has_side_effects=True, vmem_limit_bytes=44 * 1024 * 1024),
        cost_estimate=pl.CostEstimate(flops=60_000_000, bytes_accessed=4_000_000, transcendentals=0),
    )(start_states, base_flow)


def solution(mesh):
    in_specs = (P("seg", None, "gx", None, None), P("seg", None, None, "gx", None, None))
    out_specs = P("seg", None, "gx", None, None)
    body = functools.partial(local, mesh.shape["seg"], mesh.shape["gx"])
    return jax.shard_map(body, mesh=mesh, in_specs=in_specs, out_specs=out_specs, check_vma=False)
```

time: 92.5 us -> 39.2 us (0.42)
  the two profiles are of different devices: /device:TPU:0 before, /device:TPU:15 now
where the time goes in v1:
time: 39.2 us; the launch traced here: 39 us
  Pallas kernels  35.6 us (91%)
  local copies, waits for them, and re-layouts  3.4 us (9%)
    pallas_call x1, Pallas kernels, local(): pl.pallas_call(functools.partial(kernel, n_seg, n_gx, steps, nl, ny, nz),...  35.6 us
    unnamed x5, local copies, waits for them, and re-layouts  3.4 us

profile of v1, /device:TPU:15, one launch (start us, length us, event | category | flops | bytes accessed | tf_op | source)
XLA Modules:
  0.0 39.0 jit_solution(16270710374703003408)
XLA Ops:
  0.0 0.0 copy-start
  0.0 1.3 %copy-done = bf16[1,3,3,3,64,384]{5,4,3,2,1,0:T(8,128)(2,1)S(1)} copy-done((bf16[1,3,3,3,64,384]{5,4,3,2,1,0:T(8,128)(2,1)S(1)}, bf16[1,3,3,3,64,384]{5,4,3,2,1,0:T(8,128)(2,1)}, u32[]{:S(2)}) %copy-start) | copy-done | bytes 1327128
  1.3 0.0 copy-start.1
  1.3 1.2 %copy-done.1 = f32[1,3,3,64,384]{4,3,2,1,0:T(8,128)S(1)} copy-done((f32[1,3,3,64,384]{4,3,2,1,0:T(8,128)S(1)}, f32[1,3,3,64,384]{4,3,2,1,0:T(8,128)}, u32[]{:S(2)}) %copy-start.1) | copy-done | bytes 884760
  2.5 35.6 %shard_map.28 = f32[1,3,3,64,384]{4,3,2,1,0:T(8,128)S(1)} custom-call(f32[1,3,3,64,384]{4,3,2,1,0:T(8,128)S(1)} %copy-done.1, bf16[1,3,3,3,64,384]{5,4,3,2,1,0:T(8,128)(2,1)S(1)} %copy-done), custom_call_target="tpu_custom_call" | custom-call | flops 60000000 | bytes 4000000 | tf_op jit(solution)/shard_map/pallas_call | solution.py:283
  38.1 0.9 %copy.4 = f32[1,3,3,64,384]{4,3,2,1,0:T(8,128)} copy(f32[1,3,3,64,384]{4,3,2,1,0:T(8,128)S(1)} %shard_map.28) | data formatting | bytes 1769472
Async XLA Ops:
  0.0 1.3 %copy-start = (bf16[1,3,3,3,64,384]{5,4,3,2,1,0:T(8,128)(2,1)S(1)}, bf16[1,3,3,3,64,384]{5,4,3,2,1,0:T(8,128)(2,1)}, u32[]{:S(2)}) copy-start(bf16[1,3,3,3,64,384]{5,4,3,2,1,0:T(8,128)(2,1)} %base_ref.1) | copy-start | bytes 3981316
  1.3 1.2 %copy-start.1 = (f32[1,3,3,64,384]{4,3,2,1,0:T(8,128)S(1)}, f32[1,3,3,64,384]{4,3,2,1,0:T(8,128)}, u32[]{:S(2)}) copy-start(f32[1,3,3,64,384]{4,3,2,1,0:T(8,128)} %start_ref.1) | copy-start | bytes 2654212

commit v2 on v1

--- a/solution.py
+++ b/solution.py
@@ -92,15 +92,16 @@
         b[:, c, :, 0:PAD_B, :] = -wall
         b[:, c, :, PAD_B + ny:, :] = wall
 
+    pl.semaphore_wait(barrier, 3 + n_seg - 1)
+    for side in range(2):
+        b_copy(0, side).start()
     load_q.wait()
     for c in range(3):
         sq[0, 0, c] = q[0, c, nl - 1, PAD_Q:PAD_Q + ny, :].astype(BF16)
         sq[0, 1, c] = q[0, c, 0, PAD_Q:PAD_Q + ny, :].astype(BF16)
 
-    pl.semaphore_wait(barrier, 3 + n_seg - 1)
     for side in range(2):
         q_copy(0, side).start()
-        b_copy(0, side).start()
 
     @pl.when(seg == 0)
     def _():
@@ -136,15 +137,11 @@
 
             def q_side(c, side):
                 neighbour = x + (-1 if side == 0 else 1)
-                if 0 <= neighbour < nl:
-                    return q[slot, c, neighbour, pl.ds(at + PAD_Q, ROWS), :]
-                return hq[k, side, c, here, :].astype(F32)
+                return q[slot, c, neighbour, pl.ds(at + PAD_Q, ROWS), :]
 
             def b_side(c, side):
                 neighbour = x + (-1 if side == 0 else 1)
-                if 0 <= neighbour < nl:
-                    return b[k, c, neighbour, pl.ds(at + PAD_B, ROWS), :].astype(F32)
-                return hb[k, side, c, here, :].astype(F32)
+                return b[k, c, neighbour, pl.ds(at + PAD_B, ROWS), :].astype(F32)
 
             windows = [b[k, c, x, pl.ds(at, ROWS + 2 * PAD_B), :].astype(F32) for c in range(3)]
             carried = [half * window[PAD_B:PAD_B + ROWS] for window in windows]
@@ -156,23 +153,46 @@
                 centre, window = q_window(slot, c, x, at)
                 up, down = shifted(window, PAD_Q)
                 total = (1.0 - 6.0 * diffuse) * centre
-                total += ahead[0] * q_side(c, 1) + behind[0] * q_side(c, 0)
+                if x < nl - 1:
+                    total += ahead[0] * q_side(c, 1) - pushed[0] * b_side(c, 1)
+                if x > 0:
+                    total += behind[0] * q_side(c, 0) + pushed[0] * b_side(c, 0)
                 total += ahead[1] * up + behind[1] * down
                 total += ahead[2] * pltpu.roll(centre, nz - 1, 1) + behind[2] * pltpu.roll(centre, 1, 1)
-                total -= pushed[0] * (b_side(c, 1) - b_side(c, 0))
                 base = windows[c][PAD_B - 8:PAD_B + ROWS + 8]
                 up, down = shifted(base, 8)
                 total -= pushed[1] * (up - down)
                 base = windows[c][PAD_B:PAD_B + ROWS]
                 total -= pushed[2] * (pltpu.roll(base, nz - 1, 1) - pltpu.roll(base, 1, 1))
                 if k == steps - 1:
-                    out_ref[0, c, x, here, :] = total - tgt[c, x, here, :]
+                    out_ref[0, c, x, here, :] = total
                 else:
                     q[1 - slot, c, x, pl.ds(at + PAD_Q, ROWS), :] = total
-                    if x == nl - 1:
-                        sq[k + 1, 0, c, here, :] = total.astype(BF16)
-                    if x == 0:
-                        sq[k + 1, 1, c, here, :] = total.astype(BF16)
+            return carry
+
+        lax.fori_loop(0, ny // ROWS, chunk, 0)
+
+    def close(k, side):
+        slot = k % 2
+        x = 0 if side == 0 else nl - 1
+
+        def chunk(r, carry):
+            at = pl.multiple_of(r * ROWS, ROWS)
+            here = pl.ds(at, ROWS)
+            inner = pl.ds(at + PAD_Q, ROWS)
+            carried = half * b[k, 0, x, pl.ds(at + PAD_B, ROWS), :].astype(F32)
+            pushed = half * q[slot, 0, x, inner, :]
+            weight = diffuse + carried if side == 0 else diffuse - carried
+            for c in range(3):
+                gained = weight * hq[k, side, c, here, :].astype(F32)
+                pressed = pushed * hb[k, side, c, here, :].astype(F32)
+                gained = gained + pressed if side == 0 else gained - pressed
+                if k == steps - 1:
+                    out_ref[0, c, x, here, :] += gained - tgt[c, x, here, :]
+                else:
+                    total = q[1 - slot, c, x, inner, :] + gained
+                    q[1 - slot, c, x, inner, :] = total
+                    sq[k + 1, 1 - side, c, here, :] = total.astype(BF16)
             return carry
 
         lax.fori_loop(0, ny // ROWS, chunk, 0)
@@ -210,16 +230,15 @@
 
     for k in range(steps):
         load_b[k].wait()
-        if k == steps - 1:
-            finish_target()
-            for x in range(1, nl - 1):
-                layer(k, x)
+        for x in range(nl):
+            layer(k, x)
+        for side in range(2):
+            q_copy(k, side).wait_send()
+            b_copy(k, side).wait_send()
+        if k + 1 < steps:
+            for side in range(2):
+                b_copy(k + 1, side).start()
         if k == 0:
-            for x in range(1, nl - 1):
-                layer(k, x)
-            for side in range(2):
-                b_copy(1, side).start()
-
             @pl.when(seg == 0)
             def _():
                 z_copy(enc.at[0]).start()
@@ -229,21 +248,18 @@
                 a_copy(0).wait_recv()
                 z_copy(ra).start()
 
+        if k == steps - 1:
+            finish_target()
+            for x in range(1, nl - 1):
+                for c in range(3):
+                    out_ref[0, c, x] -= tgt[c, x]
         for side in range(2):
             q_copy(k, side).wait_recv()
             b_copy(k, side).wait_recv()
-        layer(k, 0)
-        layer(k, nl - 1)
-        if k < steps - 1:
-            for side in range(2):
-                q_copy(k + 1, side).start()
-            if k + 2 < steps:
-                for side in range(2):
-                    b_copy(k + 2, side).start()
-        if 0 < k < steps - 1:
-            for x in range(1, nl - 1):
-                layer(k, x)
-
+            close(k, side)
+            if k < steps - 1:
+                q_copy(k + 1, 1 - side).start()
+        if k == steps - 2:
             @pl.when(is_relay() & (seg != last))
             def _():
                 z_copy(ra).wait_recv()
@@ -251,11 +267,6 @@
                     @pl.when(seg == relays[j])
                     def _():
                         c_copy(j).start()
-
-    for k in range(steps):
-        for side in range(2):
-            q_copy(k, side).wait_send()
-            b_copy(k, side).wait_send()
 
     @pl.when(seg > 0)
     def _():
@@ -283,7 +294,7 @@
     return pl.pallas_call(
         functools.partial(kernel, n_seg, n_gx, steps, nl, ny, nz),
         out_shape=jax.ShapeDtypeStruct(start_states.shape, F32),
-        in_specs=[pl.BlockSpec(memory_space=pl.ANY)] * 2,
+        in_specs=[pl.BlockSpec(memory_space=pltpu.HBM)] * 2,
         out_specs=pl.BlockSpec(memory_space=pltpu.VMEM),
         scratch_shapes=[
             pltpu.VMEM((2, 3, nl, ny + 2 * PAD_Q, nz), F32),
@@ -305,7 +316,7 @@
             dma((1,)), dma((3,)),
         ],
         compiler_params=pltpu.CompilerParams(
-            collective_id=0, has_side_effects=True, vmem_limit_bytes=44 * 1024 * 1024),
+            collective_id=0, has_side_effects=True, vmem_limit_bytes=60 * 1024 * 1024),
         cost_estimate=pl.CostEstimate(flops=60_000_000, bytes_accessed=4_000_000, transcendentals=0),
     )(start_states, base_flow)
 

time: 39.2 us -> 34.8 us (0.89)
  Pallas kernels: 35.6 us -> 32.5 us
  local copies, waits for them, and re-layouts: 3.4 us -> 2.14 us
    pallas_call x1, Pallas kernels: 35.6 us -> 32.5 us  [local(): pl.pallas_call(functools.partial(kernel, n_seg, n_gx, steps, nl, ny, nz),...]
    unnamed x5 -> x1, local copies, waits for them, and re-layouts: 3.4 us -> 2.14 us
where the time goes in v2:
time: 34.8 us; the launch traced here: 34.6 us
  Pallas kernels  32.5 us (93%)
  local copies, waits for them, and re-layouts  2.14 us (6%)
    pallas_call x1, Pallas kernels, local(): pl.pallas_call(functools.partial(kernel, n_seg, n_gx, steps, nl, ny, nz),...  32.5 us
    unnamed x1, local copies, waits for them, and re-layouts  2.14 us

profile of v2, /device:TPU:15, one launch (start us, length us, event | category | flops | bytes accessed | tf_op | source)
XLA Modules:
  0.0 34.6 jit_solution(12028353282859317896)
XLA Ops:
  0.0 32.5 %shard_map.28 = f32[1,3,3,64,384]{4,3,2,1,0:T(8,128)} custom-call(f32[1,3,3,64,384]{4,3,2,1,0:T(8,128)} %start_ref.1, bf16[1,3,3,3,64,384]{5,4,3,2,1,0:T(8,128)(2,1)} %base_ref.1), custom_call_target="tpu_custom_call" | custom-call | flops 60000000 | bytes 4000000 | tf_op jit(solution)/shard_map/pallas_call | solution.py:294
  32.5 2.1 %copy.4 = f32[1,3,3,64,384]{4,3,2,1,0:T(8,128)} copy(f32[1,3,3,64,384]{4,3,2,1,0:T(8,128)} %shard_map.28) | data formatting | bytes 1769472

commit v3 on v2

--- a/solution.py
+++ b/solution.py
@@ -11,6 +11,7 @@
 VISCOSITY = 0.45
 MESH = pl.DeviceIdType.MESH
 ROWS = 16
+EXCHANGED = (0,)
 PAD_Q = 8
 PAD_B = 16
 F32 = jnp.float32
@@ -31,7 +32,7 @@
 
 
 def kernel(n_seg, n_gx, steps, nl, ny, nz, start_ref, base_ref, out_ref, q, b, hq, hb, sq, enc, ra, rb, tq, tgt,
-           load_sem, qs_sem, qr_sem, bs_sem, br_sem, shift_sem, a_sem, ar_sem, b_sem, c_sem, cr_sem):
+           load_sem, qs_sem, qr_sem, fs_sem, fr_sem, bs_sem, br_sem, shift_sem, a_sem, ar_sem, b_sem, c_sem, cr_sem):
     seg = lax.axis_index("seg")
     gx = lax.axis_index("gx")
     last = n_seg - 1
@@ -55,14 +56,24 @@
     for d in range(1, n_seg):
         pl.semaphore_signal(barrier, inc=1, device_id={"seg": lax.rem(seg + d, n_seg)}, device_id_type=MESH)
 
+    def comps(k):
+        return pl.ds(0, 1 if k in EXCHANGED else 3)
+
     def q_copy(k, side):
         return pltpu.make_async_remote_copy(
-            src_ref=sq.at[k, side], dst_ref=hq.at[k, side], send_sem=qs_sem.at[k, side], recv_sem=qr_sem.at[k, side],
+            src_ref=sq.at[k, side, comps(k)], dst_ref=hq.at[k, side, comps(k)],
+            send_sem=qs_sem.at[k, side], recv_sem=qr_sem.at[k, side],
             device_id={"gx": right if side == 0 else left}, device_id_type=MESH)
 
+    def f_copy(k, side):
+        return pltpu.make_async_remote_copy(
+            src_ref=sq.at[k, side, pl.ds(1, 2)], dst_ref=hq.at[k, side, pl.ds(1, 2)],
+            send_sem=fs_sem.at[k, side], recv_sem=fr_sem.at[k, side],
+            device_id={"gx": right if side == 0 else left}, device_id_type=MESH)
+
     def b_copy(k, side):
         return pltpu.make_async_remote_copy(
-            src_ref=base_ref.at[0, k, :, nl - 1 if side == 0 else 0], dst_ref=hb.at[k, side],
+            src_ref=base_ref.at[0, k, comps(k), nl - 1 if side == 0 else 0], dst_ref=hb.at[k, side, comps(k)],
             send_sem=bs_sem.at[k, side], recv_sem=br_sem.at[k, side],
             device_id={"gx": right if side == 0 else left}, device_id_type=MESH)
 
@@ -92,15 +103,13 @@
         b[:, c, :, 0:PAD_B, :] = -wall
         b[:, c, :, PAD_B + ny:, :] = wall
 
+    load_q.wait()
+    for c in range(1 if 0 in EXCHANGED else 3):
+        sq[0, 0, c] = q[0, c, nl - 1, PAD_Q:PAD_Q + ny, :].astype(BF16)
+        sq[0, 1, c] = q[0, c, 0, PAD_Q:PAD_Q + ny, :].astype(BF16)
     pl.semaphore_wait(barrier, 3 + n_seg - 1)
     for side in range(2):
         b_copy(0, side).start()
-    load_q.wait()
-    for c in range(3):
-        sq[0, 0, c] = q[0, c, nl - 1, PAD_Q:PAD_Q + ny, :].astype(BF16)
-        sq[0, 1, c] = q[0, c, 0, PAD_Q:PAD_Q + ny, :].astype(BF16)
-
-    for side in range(2):
         q_copy(0, side).start()
 
     @pl.when(seg == 0)
@@ -184,15 +193,38 @@
             pushed = half * q[slot, 0, x, inner, :]
             weight = diffuse + carried if side == 0 else diffuse - carried
             for c in range(3):
-                gained = weight * hq[k, side, c, here, :].astype(F32)
-                pressed = pushed * hb[k, side, c, here, :].astype(F32)
-                gained = gained + pressed if side == 0 else gained - pressed
+                gained = hq[k, side, c, here, :].astype(F32)
+                if c == 0 or k not in EXCHANGED:
+                    pressed = pushed * hb[k, side, c, here, :].astype(F32)
+                    gained = weight * gained + pressed if side == 0 else weight * gained - pressed
                 if k == steps - 1:
                     out_ref[0, c, x, here, :] += gained - tgt[c, x, here, :]
                 else:
                     total = q[1 - slot, c, x, inner, :] + gained
                     q[1 - slot, c, x, inner, :] = total
-                    sq[k + 1, 1 - side, c, here, :] = total.astype(BF16)
+                    if c == 0 or k + 1 not in EXCHANGED:
+                        sq[k + 1, 1 - side, c, here, :] = total.astype(BF16)
+            return carry
+
+        lax.fori_loop(0, ny // ROWS, chunk, 0)
+
+    def contribute(k, side):
+        slot = k % 2
+        x = 0 if side == 0 else nl - 1
+
+        def chunk(r, carry):
+            at = pl.multiple_of(r * ROWS, ROWS)
+            here = pl.ds(at, ROWS)
+            carried = half * hb[k, side, 0, here, :].astype(F32)
+            pushed = half * hq[k, side, 0, here, :].astype(F32)
+            for c in range(1, 3):
+                mine = q[slot, c, x, pl.ds(at + PAD_Q, ROWS), :]
+                base = b[k, c, x, pl.ds(at + PAD_B, ROWS), :].astype(F32)
+                if side == 0:
+                    share = (diffuse - carried) * mine - pushed * base
+                else:
+                    share = (diffuse + carried) * mine + pushed * base
+                sq[k, 1 - side, c, here, :] = share.astype(BF16)
             return carry
 
         lax.fori_loop(0, ny // ROWS, chunk, 0)
@@ -228,25 +260,50 @@
                         flipped = -flipped
                     tgt[c, :, j * quarter:(j + 1) * quarter, :] = flipped.reshape(nl, quarter, nz)
 
-    for k in range(steps):
-        load_b[k].wait()
-        for x in range(nl):
-            layer(k, x)
+    def start_relay():
+        @pl.when(seg == 0)
+        def _():
+            z_copy(enc.at[0]).start()
+
+        @pl.when((seg != 0) & is_relay())
+        def _():
+            a_copy(0).wait_recv()
+            z_copy(ra).start()
+
+    def sent(k):
         for side in range(2):
             q_copy(k, side).wait_send()
             b_copy(k, side).wait_send()
         if k + 1 < steps:
             for side in range(2):
                 b_copy(k + 1, side).start()
+
+    def arrived(k, side):
+        q_copy(k, side).wait_recv()
+        b_copy(k, side).wait_recv()
+
+    for k in range(steps):
+        load_b[k].wait()
+        exchanged = k in EXCHANGED
+        for x in range(nl):
+            layer(k, x)
+            if exchanged and x == nl - 2:
+                sent(k)
+        if exchanged:
+            for side in range(2):
+                arrived(k, side)
+                contribute(k, side)
+                f_copy(k, 1 - side).start()
+        else:
+            sent(k)
         if k == 0:
-            @pl.when(seg == 0)
-            def _():
-                z_copy(enc.at[0]).start()
-
-            @pl.when((seg != 0) & is_relay())
-            def _():
-                a_copy(0).wait_recv()
-                z_copy(ra).start()
+            if exchanged:
+                for side in range(2):
+                    f_copy(k, side).wait_send()
+            start_relay()
+        elif exchanged:
+            for side in range(2):
+                f_copy(k, side).wait_send()
 
         if k == steps - 1:
             finish_target()
@@ -254,8 +311,10 @@
                 for c in range(3):
                     out_ref[0, c, x] -= tgt[c, x]
         for side in range(2):
-            q_copy(k, side).wait_recv()
-            b_copy(k, side).wait_recv()
+            if exchanged:
+                f_copy(k, side).wait_recv()
+            else:
+                arrived(k, side)
             close(k, side)
             if k < steps - 1:
                 q_copy(k + 1, 1 - side).start()
@@ -310,15 +369,16 @@
             dma((1 + steps,)),
             dma((steps, 2)), dma((steps, 2)),
             dma((steps, 2)), dma((steps, 2)),
+            dma((steps, 2)), dma((steps, 2)),
             dma((2,)),
             dma((4,)), dma((1,)),
             dma((2,)),
             dma((1,)), dma((3,)),
         ],
         compiler_params=pltpu.CompilerParams(
-            collective_id=0, has_side_effects=True, vmem_limit_bytes=60 * 1024 * 1024),
+            collective_id=0, has_side_effects=True, vmem_limit_bytes=44 * 1024 * 1024),
         cost_estimate=pl.CostEstimate(flops=60_000_000, bytes_accessed=4_000_000, transcendentals=0),
-    )(start_states, base_flow)
+    )(pltpu.with_memory_space_constraint(start_states, pltpu.HBM), pltpu.with_memory_space_constraint(base_flow, pltpu.HBM))
 
 
 def solution(mesh):

time: 34.8 us -> 30.7 us (0.88)
  Pallas kernels: 32.5 us -> 29.3 us
  local copies, waits for them, and re-layouts: 2.14 us -> 0.91 us
    pallas_call x1, Pallas kernels: 32.5 us -> 29.3 us  [local(): pl.pallas_call(functools.partial(kernel, n_seg, n_gx, steps, nl, ny, nz),...]
    unnamed x1, local copies, waits for them, and re-layouts: 2.14 us -> 0.91 us
where the time goes in v3:
time: 30.7 us; the launch traced here: 30.2 us
  Pallas kernels  29.3 us (95%)
  local copies, waits for them, and re-layouts  0.91 us (3%)
    pallas_call x1, Pallas kernels, local(): pl.pallas_call(functools.partial(kernel, n_seg, n_gx, steps, nl, ny, nz),...  29.3 us
    unnamed x1, local copies, waits for them, and re-layouts  0.91 us

profile of v3, /device:TPU:15, one launch (start us, length us, event | category | flops | bytes accessed | tf_op | source)
XLA Modules:
  0.0 30.2 jit_solution(10141403903871456545)
XLA Ops:
  0.0 29.3 %shard_map.28 = f32[1,3,3,64,384]{4,3,2,1,0:T(8,128)S(1)} custom-call(f32[1,3,3,64,384]{4,3,2,1,0:T(8,128)} %start_ref.1, bf16[1,3,3,3,64,384]{5,4,3,2,1,0:T(8,128)(2,1)} %base_ref.1), custom_call_target="tpu_custom_call" | custom-call | flops 60000000 | bytes 4000000 | tf_op jit(solution)/shard_map/pallas_call | solution.py:353
  29.3 0.9 %copy.4 = f32[1,3,3,64,384]{4,3,2,1,0:T(8,128)} copy(f32[1,3,3,64,384]{4,3,2,1,0:T(8,128)S(1)} %shard_map.28) | data formatting | bytes 1769472
